TPU v7x, 32 devices: a whole 2x2x4 slice. The times are simulated.
32 devices in a mesh: dp: 4 (over y, x), row: 4 (over z), col: 2 (over core).
Axes of the slice: x: 2, y: 2, z: 4, core: 2. Of those that a mesh axis runs over, the one named last changes fastest.
Arguments:
- inputs: bfloat16 [2916, 1152], P('dp', ('row', 'col')), may hold values from -11 to 11
- cotangent: bfloat16 [2916, 1152], P('dp', ('row', 'col')), may hold values from -6 to 6
- qkv_master: float32 [288, 4, 3456], P('row', 'dp', 'col'), may hold values from -0.1875 to 0.1875
- out_master: float32 [1152, 288, 4], P('col', 'row', 'dp'), may hold values from -1 to 1
- up_master: float32 [288, 4, 4304], P('row', 'dp', 'col'), may hold values from -0.20623948 to 0.20623948
- down_master: float32 [4304, 288, 4], P('col', 'row', 'dp'), may hold values from -0.09375 to 0.09375
- qkv_first: float32 [288, 4, 3456], P('row', 'dp', 'col'), may hold values from -16 to 16
- out_first: float32 [1152, 288, 4], P('col', 'row', 'dp'), may hold values from -6 to 6
- up_first: float32 [288, 4, 4304], P('row', 'dp', 'col'), may hold values from -6 to 6
- down_first: float32 [4304, 288, 4], P('col', 'row', 'dp'), may hold values from -20 to 20
- qkv_second: float32 [288, 4, 3456], P('row', 'dp', 'col'), may hold values from 0.729 to 2.916
- out_second: float32 [1152, 288, 4], P('col', 'row', 'dp'), may hold values from 0.06561 to 0.26244
- up_second: float32 [288, 4, 4304], P('row', 'dp', 'col'), may hold values from 0.26244 to 1.04976
- down_second: float32 [4304, 288, 4], P('col', 'row', 'dp'), may hold values from 1.04976 to 4.19904
- norm_gains: float32 [2, 1152], replicated, may hold values from 0.5 to 1.5
- gain_first: float32 [2, 1152], replicated, may hold values from -32 to 32
- gain_second: float32 [2, 1152], replicated, may hold values from 2.916 to 11.664
- biases: float32 [11216], replicated, may hold values from -1.5 to 1.5
- bias_first: float32 [11216], replicated, may hold values from -32 to 32
- bias_second: float32 [11216], replicated, may hold values from 2.916 to 11.664
Outputs:
- outputs: bfloat16 [2916, 1152], P('dp', ('row', 'col'))
- input_grad: bfloat16 [2916, 1152], P('dp', ('row', 'col'))
- new_qkv: float32 [288, 4, 3456], P('row', 'dp', 'col')
- new_qkv_first: float32 [288, 4, 3456], P('row', 'dp', 'col')
- new_qkv_second: float32 [288, 4, 3456], P('row', 'dp', 'col')
- new_out: float32 [1152, 288, 4], P('col', 'row', 'dp')
- new_out_first: float32 [1152, 288, 4], P('col', 'row', 'dp')
- new_out_second: float32 [1152, 288, 4], P('col', 'row', 'dp')
- new_up: float32 [288, 4, 4304], P('row', 'dp', 'col')
- new_up_first: float32 [288, 4, 4304], P('row', 'dp', 'col')
- new_up_second: float32 [288, 4, 4304], P('row', 'dp', 'col')
- new_down: float32 [4304, 288, 4], P('col', 'row', 'dp')
- new_down_first: float32 [4304, 288, 4], P('col', 'row', 'dp')
- new_down_second: float32 [4304, 288, 4], P('col', 'row', 'dp')
- new_gains: float32 [2, 1152], replicated
- new_gain_first: float32 [2, 1152], replicated
- new_gain_second: float32 [2, 1152], replicated
- new_biases: float32 [11216], replicated
- new_bias_first: float32 [11216], replicated
- new_bias_second: float32 [11216], replicated
All inputs are finite; a program needn't handle non-finite values.
Results may differ from a plain program's by a relative error of at most 0.02.
Values may be sent and summed in bfloat16 or wider, within the bound.
No kernel may reach another device: no remote copies, remote signals or barrier semaphores. Data moves between devices by JAX's collectives and lax.ppermute only.
A program may use at most 128 MiB of HBM per device.

v0:
```python
import jax
import jax.numpy as jnp
from jax import lax
from jax.experimental import pallas as pl
from jax.experimental.pallas import tpu as pltpu
from jax.sharding import PartitionSpec as P

D = 1152
FF = 4304
HEAD = 72
SEQ = 729
STEP = 10

NORM_EPS = 1e-06
ADAM_EPS = 1e-08
BETA_ONE = 0.9
BETA_TWO = 0.999
LOW = jnp.bfloat16


def dot(left, right, left_dim, right_dim, out=jnp.float32, precision=None):
    return lax.dot_general(
        left,
        right,
        (((left_dim,), (right_dim,)), ((), ())),
        precision=precision,
        preferred_element_type=out,
    )


def take(array, index, size):
    return lax.dynamic_slice_in_dim(array, index * size, size, axis=0)


def swap_cores(array):
    n_col = lax.axis_size("col")
    return lax.ppermute(array, "col", [(i, (i + 1) % n_col) for i in range(n_col)])


def both_cores(rows):
    pieces = [
        lax.all_gather(piece, "col", axis=0) for piece in jnp.split(rows, 2, axis=0)
    ]
    return jnp.concatenate(pieces, axis=1).reshape(-1, rows.shape[1])


def send_copies(block, axis):
    copies = jnp.broadcast_to(block, (lax.axis_size(axis),) + block.shape)
    return lax.all_to_all(copies, axis, 0, 0).reshape(-1, block.shape[1])


def zero_of(array):
    first = lax.slice(array, (0,) * array.ndim, (1,) * array.ndim)
    return first.reshape(()).astype(jnp.float32) * 0.0


def exchange_rows(blocks):
    return lax.all_to_all(blocks, "row", 0, 0)


def all_sum(vector):
    for axis in ("col", "row", "dp"):
        size = lax.axis_size(axis)
        if size & (size - 1) or size > 4:
            vector = lax.psum(vector, axis)
            continue
        step = 1
        while step < size:
            vector = vector + lax.ppermute(vector, axis, [(i, i ^ step) for i in range(size)])
            step *= 2
    return vector


VMEM = pl.BlockSpec(memory_space=pltpu.VMEM)
SMEM = pl.BlockSpec(memory_space=pltpu.SMEM)
BIG = pltpu.CompilerParams(vmem_limit_bytes=56 * 1024 * 1024)


def head_probs(queries, key_rows):
    scores = dot(queries, key_rows, 0, 0) * HEAD ** (-0.5)
    scores = jnp.where(lax.broadcasted_iota(jnp.int32, scores.shape, 1) < SEQ, scores, -1e30)
    exponent = jnp.exp(scores - jnp.max(scores, axis=1, keepdims=True))
    return exponent * (1.0 / jnp.sum(exponent, axis=1, keepdims=True))


def split_cores(core, first, second, theirs_ref, mine_ref):
    @pl.when(core == 0)
    def _():
        mine_ref[...] = first
        theirs_ref[...] = second

    @pl.when(core != 0)
    def _():
        mine_ref[...] = second
        theirs_ref[...] = first


def attend_kernel(core_ref, w_ref, za_ref, bias_ref, out_ref, qkv_ref, att_ref, theirs_ref, mine_ref):
    qkv = dot(w_ref[...], za_ref[...], 0, 0) + bias_ref[...]
    heads = qkv_ref.shape[0]
    parts = []
    for head in range(heads):
        for t in range(3):
            start = (head * 3 + t) * HEAD
            qkv_ref[head, t] = qkv[start : start + HEAD].astype(LOW)
        probs = head_probs(qkv_ref[head, 0], qkv_ref[head, 1]).astype(LOW)
        parts.append(dot(qkv_ref[head, 2], probs, 1, 1))
    attended = jnp.concatenate(parts, axis=0).T.astype(LOW)
    att_ref[...] = attended
    branch = dot(attended, out_ref[...], 1, 1).astype(LOW)
    half = branch.shape[0] // 2
    split_cores(core_ref[0], branch[:half], branch[half:], theirs_ref, mine_ref)


def attend(core, w_qkv, za, qkv_bias, w_out):
    tokens = za.shape[1]
    width = w_out.shape[1]
    return pl.pallas_call(
        attend_kernel,
        in_specs=[SMEM, VMEM, VMEM, VMEM, VMEM],
        out_specs=[VMEM] * 4,
        out_shape=(
            jax.ShapeDtypeStruct((width // HEAD, 3, HEAD, tokens), LOW),
            jax.ShapeDtypeStruct((tokens, width), LOW),
            jax.ShapeDtypeStruct((tokens // 2, D), LOW),
            jax.ShapeDtypeStruct((tokens // 2, D), LOW),
        ),
        compiler_params=BIG,
        name="attend",
    )(core, w_qkv, za, qkv_bias, w_out)


def mlp_kernel(core_ref, zb_ref, up_ref, bias_ref, grad_ref, act_ref, hid_ref, two_ref, sum_ref):
    hidden = dot(zb_ref[...], up_ref[...], 1, 0) + bias_ref[...]
    square = hidden * hidden
    slope = 0.7978845608028654 * (1.0 + 0.044715 * square)
    bent = jnp.tanh(hidden * slope)
    gate = 0.5 * (1.0 + bent)
    act_ref[...] = (hidden * gate).astype(LOW)
    steep = gate + 0.5 * hidden * (1.0 - bent * bent) * (
        0.7978845608028654 * (1.0 + 3 * 0.044715 * square)
    )
    hidden_grad = (grad_ref[...] * steep).astype(LOW)
    hid_ref[...] = hidden_grad
    two_ref[...] = dot(hidden_grad, up_ref[...], 1, 1).astype(LOW)

    @pl.when(pl.program_id(0) == 0)
    def _():
        sum_ref[...] = jnp.zeros(sum_ref.shape, jnp.float32)

    sum_ref[...] += jnp.sum(hidden_grad.astype(jnp.float32), axis=0, keepdims=True)


def mlp(core, zb, w_up, up_bias, active_grad):
    tokens = zb.shape[0]
    wide = w_up.shape[1]
    steps = 6
    block = tokens // steps
    turned = lambda i, c: ((i + (steps // 2) * (1 - c[0])) % steps, 0)
    whole = lambda i, c: (0, 0)
    return pl.pallas_call(
        mlp_kernel,
        grid_spec=pltpu.PrefetchScalarGridSpec(
            num_scalar_prefetch=1,
            grid=(steps,),
            in_specs=[
                pl.BlockSpec((block, D), turned),
                pl.BlockSpec((D, wide), whole),
                pl.BlockSpec((1, wide), whole),
                pl.BlockSpec((block, wide), turned),
            ],
            out_specs=[
                pl.BlockSpec((block, wide), turned),
                pl.BlockSpec((block, wide), turned),
                pl.BlockSpec((block, D), lambda i, c: (i, 0)),
                pl.BlockSpec((1, wide), whole),
            ],
        ),
        out_shape=(
            jax.ShapeDtypeStruct((tokens, wide), LOW),
            jax.ShapeDtypeStruct((tokens, wide), LOW),
            jax.ShapeDtypeStruct((tokens, D), LOW),
            jax.ShapeDtypeStruct((1, wide), jnp.float32),
        ),
        compiler_params=BIG,
        name="mlp",
    )(core, zb, w_up, up_bias, active_grad)


def back_kernel(bg_ref, out_ref, qkv_ref, za_ref, att_ref, grad_ref, sum_ref, wq_ref, wo_ref):
    attended_grad = dot(bg_ref[...], out_ref[...], 1, 0).T
    scale = HEAD ** (-0.5)
    parts = []
    for head in range(qkv_ref.shape[0]):
        queries, key_rows, values = qkv_ref[head, 0], qkv_ref[head, 1], qkv_ref[head, 2]
        grad = attended_grad[head * HEAD : (head + 1) * HEAD].astype(LOW)
        probs = head_probs(queries, key_rows)
        probs_grad = dot(grad, values, 0, 0)
        inner = jnp.sum(probs * probs_grad, axis=1, keepdims=True)
        scores_grad = (probs * (probs_grad - inner)).astype(LOW)
        parts.append(dot(key_rows, scores_grad, 1, 1) * scale)
        parts.append(dot(queries, scores_grad, 1, 0) * scale)
        parts.append(dot(grad, probs.astype(LOW), 1, 0))
    qkv_grad = jnp.concatenate(parts, axis=0).astype(LOW)
    grad_ref[...] = qkv_grad
    sum_ref[...] = jnp.sum(qkv_grad.astype(jnp.float32), axis=1, keepdims=True)
    wq_ref[...] = dot(za_ref[...], qkv_grad, 1, 1).astype(LOW)
    wo_ref[...] = dot(bg_ref[...], att_ref[...], 0, 0).astype(LOW)


def attend_back(branch_all, w_out, qkv, za, attended):
    tokens = za.shape[1]
    width = w_out.shape[1]
    return pl.pallas_call(
        back_kernel,
        in_specs=[VMEM] * 5,
        out_specs=[VMEM] * 4,
        out_shape=(
            jax.ShapeDtypeStruct((3 * width, tokens), LOW),
            jax.ShapeDtypeStruct((3 * width, 1), jnp.float32),
            jax.ShapeDtypeStruct((D, 3 * width), LOW),
            jax.ShapeDtypeStruct((D, width), LOW),
        ),
        compiler_params=BIG,
        name="attend_back",
    )(branch_all, w_out, qkv, za, attended)


def first_kernel(core_ref, w_ref, grad_ref, x_ref, mean_ref, inv_ref, gain_ref, theirs_ref, mine_ref, sum_ref):
    n_row, rows, tokens = theirs_ref.shape
    width = rows - 16
    first = jnp.zeros((1, tokens), jnp.float32)
    second = jnp.zeros((1, tokens), jnp.float32)
    blocks = []
    for slot in range(D // width):
        here = slice(slot * width, (slot + 1) * width)
        part = dot(w_ref[here], grad_ref[...], 1, 0)
        normed = (x_ref[here].astype(jnp.float32) - mean_ref[...]) * inv_ref[...]
        product = part * normed
        sum_ref[here, 0:1] = jnp.sum(product, axis=1, keepdims=True)
        sum_ref[here, 1:2] = jnp.sum(part, axis=1, keepdims=True)
        first += jnp.sum(part * gain_ref[here], axis=0, keepdims=True)
        second += jnp.sum(product * gain_ref[here], axis=0, keepdims=True)
        blocks.append(part.astype(LOW))
    line = lax.broadcasted_iota(jnp.int32, (16, tokens), 0)
    sums = jnp.where(line == 0, first, jnp.where(line == 1, second, 0.0)).astype(LOW)
    for near, ref in ((False, theirs_ref), (True, mine_ref)):
        for core in range(2):

            @pl.when((core_ref[0] == core) == near)
            def _(core=core, ref=ref):
                for row in range(n_row):
                    ref[row, :width] = blocks[core * n_row + row]
                    ref[row, width:] = sums


def first_back(core, w_mixed, qkv_grad, x_all, x_mean, inverse, gain, width, n_row):
    tokens = x_all.shape[1]
    return pl.pallas_call(
        first_kernel,
        in_specs=[SMEM] + [VMEM] * 6,
        out_specs=[VMEM] * 3,
        out_shape=(
            jax.ShapeDtypeStruct((n_row, width + 16, tokens), LOW),
            jax.ShapeDtypeStruct((n_row, width + 16, tokens), LOW),
            jax.ShapeDtypeStruct((D, 2), jnp.float32),
        ),
        compiler_params=BIG,
        name="first_back",
    )(core, w_mixed, qkv_grad, x_all, x_mean, inverse, gain)


def adam_update(weights, moment_one, second, gradient, step_rate, weight_decay):
    moment_one = BETA_ONE * moment_one + (1.0 - BETA_ONE) * gradient
    second = BETA_TWO * second + (1.0 - BETA_TWO) * gradient * gradient
    direction = (
        moment_one / (1.0 - BETA_ONE**STEP) / (jnp.sqrt(second / (1.0 - BETA_TWO**STEP)) + ADAM_EPS)
    )
    return (weights - step_rate * (direction + weight_decay * weights), moment_one, second)


def shards(
    inputs,
    cotangent,
    qkv_master,
    out_master,
    up_master,
    down_master,
    qkv_first,
    out_first,
    up_first,
    down_first,
    qkv_second,
    out_second,
    up_second,
    down_second,
    norm_gains,
    gain_first,
    gain_second,
    biases,
    bias_first,
    bias_second,
):
    tokens, width = inputs.shape
    n_row = lax.axis_size("row")
    n_col = lax.axis_size("col")
    n_dp = lax.axis_size("dp")
    row = lax.axis_index("row")
    core = lax.axis_index("col")
    core_of = core.reshape(1).astype(jnp.int32)
    group = n_row * n_col
    heads = width // HEAD
    hidden_width = FF // group
    own = core * n_row + row
    padded = -(-tokens // (group * 16)) * (group * 16)
    half = padded // n_col
    shard_rows = qkv_master.shape[0]

    place = lax.broadcasted_iota(jnp.int32, (D, D), 0)
    source = lax.broadcasted_iota(jnp.int32, (D, D), 1)
    feature = (
        ((place // width) % n_row) * n_col + place // (width * n_row)
    ) * width + place % width
    order = lax.optimization_barrier(
        (source == (feature % n_dp) * (D // n_dp) + feature // n_dp).astype(LOW)
    )

    def mixed(vector):
        return vector.reshape(n_row, n_col, width).transpose(1, 0, 2).reshape(D)

    def plain(vector):
        return vector.reshape(n_col, n_row, width).transpose(1, 0, 2).reshape(D)

    def dealt(vector):
        return vector.reshape(D // n_dp, n_dp).T.reshape(D)

    def undealt(vector):
        return vector.reshape(n_dp, D // n_dp).T.reshape(D)

    def to_owner(rows, parts):
        return rows.reshape(shard_rows, parts, -1).transpose(1, 0, 2)

    def scattered(gradient):
        return lax.psum_scatter(gradient, "dp", scatter_dimension=0, tiled=True)

    def returned(rows):
        blocks = exchange_rows(rows.reshape(n_row, shard_rows, -1))
        return blocks.astype(jnp.float32)

    def widened(blocks):
        return blocks.transpose(1, 0, 2).reshape(shard_rows, -1)

    def long(array):
        return jnp.pad(array, ((0, 0), (0, padded - tokens)))

    qkv_rows = exchange_rows(to_owner(qkv_master[:, 0].astype(LOW), n_row))
    x_own = long(inputs.T)
    x_all = both_cores(lax.all_gather(x_own, "row", axis=0, tiled=True))
    w_qkv = send_copies(qkv_rows.reshape(D // n_dp, -1), "dp")
    rest = jnp.concatenate(
        [
            to_owner(out_master[:, :, 0].T.astype(LOW), n_row),
            to_owner(up_master[:, 0].astype(LOW), n_row),
            to_owner(down_master[:, :, 0].T.astype(LOW), n_row),
        ],
        axis=2,
    )
    rest = exchange_rows(rest).reshape(D // n_dp, -1)
    w_out = lax.all_gather(rest[:, :width], "dp", axis=0, tiled=True)
    w_up = lax.all_gather(rest[:, width : width + hidden_width], "dp", axis=0, tiled=True)
    w_down = lax.all_gather(rest[:, width + hidden_width :], "dp", axis=0, tiled=True)
    cot_all = lax.all_gather(long(cotangent.T), ("row", "col"), axis=0, tiled=True)

    gain_one = mixed(norm_gains[0])
    gain_two = dealt(norm_gains[1])
    shift_one = mixed(biases[:D])
    shift_two = dealt(biases[D : 2 * D])
    query_bias = lax.dynamic_slice_in_dim(biases, 2 * D + own * width, width).reshape(heads, HEAD)
    value_bias = lax.dynamic_slice_in_dim(biases, 3 * D + own * width, width).reshape(heads, HEAD)
    out_bias = dealt(biases[4 * D : 5 * D])
    feature_start = (row * n_col + core) * width
    down_bias = lax.dynamic_slice_in_dim(biases, 5 * D + feature_start, width)
    up_bias = lax.dynamic_slice_in_dim(biases, 6 * D + own * hidden_width, hidden_width)
    qkv_bias = jnp.stack([query_bias, jnp.zeros_like(query_bias), value_bias], axis=1).reshape(
        3 * width, 1
    )

    x_full = x_all.astype(jnp.float32)
    x_mean = jnp.sum(x_full, axis=0, keepdims=True) / D
    center = x_full - x_mean
    inverse_one = lax.rsqrt(jnp.sum(center * center, axis=0, keepdims=True) / D + NORM_EPS)
    za = (center * inverse_one * gain_one[:, None] + shift_one[:, None]).astype(LOW)
    za = dot(order, za, 0, 0, LOW)

    qkv, attended, theirs, mine = attend(core_of, w_qkv, za, qkv_bias, w_out)
    pair = (mine.astype(jnp.float32) + swap_cores(theirs).astype(jnp.float32)).astype(LOW)
    branch = lax.psum(pair, "row").astype(jnp.float32)

    x_half = lax.dynamic_slice_in_dim(x_all, core * half, half, axis=1)
    x_half = dot(x_half, order, 0, 0)
    cot_mixed = cot_all.reshape(n_row, n_col, width, padded).transpose(1, 0, 2, 3)
    cot_tokens = dot(cot_mixed.reshape(D, padded), order, 0, 0, LOW)
    active_grad = dot(cot_tokens, w_down, 1, 0)
    cot_half = take(cot_tokens, core, half).astype(jnp.float32)
    qkv_mixed = dot(order, w_qkv, 1, 0, LOW)
    down_mixed = dot(order, w_down, 1, 0, LOW)

    middle = x_half + branch + out_bias[None, :]
    center = middle - jnp.sum(middle, axis=1, keepdims=True) / D
    inverse_two = lax.rsqrt(jnp.sum(center * center, axis=1, keepdims=True) / D + NORM_EPS)
    normed_two = center * inverse_two
    zb = both_cores((normed_two * gain_two + shift_two).astype(LOW))

    active, hidden_grad, two_parts, up_sums = mlp(core_of, zb, w_up, up_bias[None, :], active_grad)
    pair = two_parts[half:].astype(jnp.float32) + swap_cores(two_parts[:half]).astype(jnp.float32)
    two_grad = lax.psum(pair.astype(LOW), "row").astype(jnp.float32)
    down_rows = scattered(dot(cot_tokens, active, 0, 0, LOW))
    up_rows = scattered(dot(zb, hidden_grad, 0, 0, LOW))

    scaled = two_grad * gain_two
    first_sum = jnp.sum(scaled, axis=1, keepdims=True) / D
    second_sum = jnp.sum(scaled * normed_two, axis=1, keepdims=True) / D
    middle_grad = cot_half + inverse_two * (scaled - first_sum - normed_two * second_sum)
    middle_grad = middle_grad.astype(LOW)
    branch_all = both_cores(middle_grad)

    qkv_grad, bias_sums, qkv_full, out_full = attend_back(branch_all, w_out, qkv, za, attended)
    theirs, mine, one_sums = first_back(
        core_of, qkv_mixed, qkv_grad, x_all, x_mean, inverse_one, gain_one[:, None], width, n_row
    )
    qkv_blocks = lax.all_to_all(qkv_full.reshape(n_dp, D // n_dp, -1), "dp", 0, 0)
    qkv_rows = jnp.sum(qkv_blocks.astype(jnp.float32), axis=0).astype(LOW)
    pair = (mine.astype(jnp.float32) + swap_cores(theirs).astype(jnp.float32)).astype(LOW)
    one_grad = jnp.sum(exchange_rows(pair).astype(jnp.float32), axis=0)
    own_gain = lax.dynamic_slice_in_dim(norm_gains[0], feature_start, width)[:, None]
    own_normed = (x_own.astype(jnp.float32) - x_mean) * inverse_one
    own_order = lax.dynamic_slice_in_dim(order, own * width, width, axis=0)
    own_middle = dot(own_order, branch_all, 1, 1)
    input_grad = own_middle + inverse_one * (
        one_grad[:width] * own_gain
        - one_grad[width : width + 1] / D
        - own_normed * (one_grad[width + 1 : width + 2] / D)
    )
    input_grad = input_grad.astype(LOW)[:, :tokens].T

    middle_mixed = dot(order, middle.astype(LOW), 1, 1)
    at_row = ((jnp.arange(D) // width) % n_row == row)[:, None]
    middle_mixed = jnp.where(at_row, middle_mixed, 0.0)
    middle_mixed = lax.dynamic_update_slice_in_dim(
        jnp.zeros((D, padded), jnp.float32), middle_mixed, core * half, 1
    )
    result = (dot(down_mixed, active, 1, 1) + middle_mixed + zero_of(branch_all)).astype(LOW)
    result = lax.psum_scatter(result, "col", scatter_dimension=0, tiled=True)
    result = exchange_rows(result.reshape(n_row, width, padded))
    result = jnp.sum(result.astype(jnp.float32), axis=0) + down_bias[:, None]
    result = result.astype(LOW)[:, :tokens].T

    out_rows = scattered(out_full)
    last = returned(jnp.concatenate([out_rows, qkv_rows], axis=1))
    out_blocks = last[:, :, :width]
    qkv_blocks = last[:, :, width:]

    bias_sums = bias_sums.reshape(heads, 3, HEAD)
    once = (row == 0).astype(jnp.float32)
    shared = jnp.stack(
        [
            jnp.sum(two_grad * normed_two, axis=0),
            jnp.sum(two_grad, axis=0),
            jnp.sum(middle_grad, axis=0, dtype=jnp.float32),
            jnp.sum(cot_half, axis=0),
        ]
    )
    shared = (shared * once).reshape(4, n_dp, D // n_dp).transpose(0, 2, 1).reshape(4, D)
    bias_grad = jnp.concatenate(
        [
            plain(one_sums[:, 0]),
            shared[0],
            plain(one_sums[:, 1]),
            shared[1],
            jnp.zeros((2 * D,), jnp.float32),
            shared[2],
            shared[3],
            jnp.zeros((FF,), jnp.float32),
        ]
    )
    for piece, offset in (
        (bias_sums[:, 0].reshape(width), 4 * D + own * width),
        (bias_sums[:, 2].reshape(width), 5 * D + own * width),
        (up_sums[0], 8 * D + own * hidden_width),
    ):
        bias_grad = lax.dynamic_update_slice_in_dim(bias_grad, piece, offset, 0)
    total = all_sum(bias_grad)
    gain_total = total[: 2 * D].reshape(2, D)
    bias_total = total[2 * D :]

    later = zero_of(qkv_grad)
    first = returned(jnp.concatenate([up_rows, down_rows], axis=1))
    up_blocks = first[:, :, :hidden_width]
    down_blocks = first[:, :, hidden_width:]
    q_new = adam_update(
        qkv_master, qkv_first, qkv_second, widened(qkv_blocks)[:, None], 0.03, 0.1
    )
    o_new = adam_update(
        out_master, out_first, out_second, widened(out_blocks).T[:, :, None], 0.12, 0.1
    )
    u_new = adam_update(
        up_master, up_first, up_second, widened(up_blocks + later)[:, None], 0.03, 0.1
    )
    d_new = adam_update(
        down_master, down_first, down_second, widened(down_blocks + later).T[:, :, None], 0.02, 0.1
    )
    g_new = adam_update(norm_gains, gain_first, gain_second, gain_total, 0.5, 0.0)
    b_new = adam_update(biases, bias_first, bias_second, bias_total, 0.5, 0.0)
    return (result, input_grad, *q_new, *o_new, *u_new, *d_new, *g_new, *b_new)


def solution(mesh):
    token_spec = P("dp", ("row", "col"))
    wide = P("row", "dp", "col")
    tall = P("col", "row", "dp")
    return jax.shard_map(
        shards,
        mesh=mesh,
        in_specs=(token_spec,) * 2 + (wide, tall, wide, tall) * 3 + (P(),) * 6,
        out_specs=(token_spec,) * 2
        + (wide,) * 3
        + (tall,) * 3
        + (wide,) * 3
        + (tall,) * 3
        + (P(),) * 6,
        check_vma=False,
    )
```

profile of v0, /device:TPU:0, one launch (start us, length us, event | category | flops | bytes accessed | tf_op | source)
XLA Modules:
  0.0 489.3 jit_solution(10716980261865066227)
XLA Ops:
  11.7 6.3 %all-to-all-start.1 = ((bf16[4,72,432]{2,1,0:T(8,128)(2,1)}), bf16[4,72,432]{2,1,0:T(8,128)(2,1)}, u32[]{:S(2)}, u32[]{:S(2)}) async-start(bf16[4,72,432]{2,1,0:T(8,128)(2,1)} %copy.119), calls=%async_computation.1 | async-start | bytes 589824 | tf_op jit(solution)/shard_map/all_to_all | solution.py:58
  20.0 22.4 %all_gather.52 = bf16[576,768]{1,0:T(8,128)(2,1)S(1)} all-gather(bf16[144,768]{1,0:T(8,128)(2,1)S(1)} %pad.7), channel_id=1, replica_groups=mesh['dp'=4,'row'=4,'col'=2] {'row'}, dimensions={0}, use_global_device_ids=true | all-gather | bytes 1105920 | tf_op jit(solution)/shard_map/all_gather | solution.py:358
  42.4 5.8 %fusion.12 = bf16[1152,1152]{1,0:T(8,128)(2,1)} fusion(s32[1152]{0:T(1024)S(1)} %get-tuple-element.188, s32[1152]{0:T(1024)S(1)} %get-tuple-element.189, s32[1152]{0:T(1024)S(1)} %get-tuple-element.186, s32[1152]{0:T(1024)S(1)} %get-tuple-element.192, s32[1152]{0:T(1024)S(1)} %get-tuple-element.187, s32[1152]{0:T(1024)S(1)} %get-tuple-element.193, ...), kind=kLoop, calls=%fused_computation.23 | loop fusion | flops 54411264 | bytes 2685312 | tf_op jit(solution)/shard_map/convert_element_type | solution.py:325
  56.4 3.6 all-to-all-start
  63.4 16.0 %all-to-all-done = bf16[4,72,1220]{2,1,0:T(8,128)(2,1)S(1)} async-done(((bf16[4,72,1220]{2,1,0:T(8,128)(2,1)}), bf16[4,72,1220]{2,1,0:T(8,128)(2,1)S(1)}, u32[]{:S(2)}, u32[]{:S(2)}) %all-to-all-start) | async-done | bytes 702752 | tf_op jit(solution)/shard_map/all_to_all | solution.py:58
  81.8 3.7 all-to-all-start.2
  85.5 5.8 %fusion.25.za_ref = bf16[1152,768]{1,0:T(8,128)(2,1)} fusion(bf16[1152,1152]{1,0:T(8,128)(2,1)} %fusion.12, bf16[1152,768]{1,0:T(8,128)(2,1)S(1)} %bitcast.123, f32[1152]{0:T(1024)S(1)} %add.335, f32[1152]{0:T(1024)S(1)} %mul.444, f32[768]{0:T(1024)S(1)} %add_rsqrt_fusion, f32[768]{0:T(1024)S(1)} %broadcast_multiply_fusion), kind=kOutput, calls=%fused_computation.48 | convolution fusion | flops 2043740160 | bytes 6208512 | tf_op jit(solution)/shard_map/dot_general | solution.py:22
  92.3 13.5 %all-gather.6 = bf16[4,288,144]{1,2,0:T(8,128)(2,1)S(1)} all-gather(bf16[1,288,144]{1,2,0:T(8,128)(2,1)S(1)} %copy.122), channel_id=1, replica_groups=mesh['dp'=4,'row'=4,'col'=2] {'dp'}, dimensions={0}, use_global_device_ids=true | all-gather | bytes 414720 | tf_op jit(solution)/shard_map/all_gather | solution.py:369
  108.0 8.4 %attend.1 = (bf16[2,3,72,768]{3,2,1,0:T(8,128)(2,1)}, bf16[768,144]{1,0:T(8,128)(2,1)}, bf16[384,1152]{1,0:T(8,128)(2,1)}, bf16[384,1152]{1,0:T(8,128)(2,1)}) custom-call(s32[1]{0:T(128)} %bitcast.6.core_ref, bf16[1152,432]{1,0:T(8,128)(2,1)} %bitcast.130, bf16[1152,768]{1,0:T(8,128)(2,1)} %fusion.25.za_ref, f32[432,1]{1,0:T(8,128)} %reshape.366.bias_ref, ...), custom_call_target="tpu_custom_call" | custom-call | tf_op jit(solution)/shard_map/attend/pallas_call | solution.py:118
  130.5 45.5 %all-reduce.5.cloned.1.call-done = bf16[384,1152]{1,0:T(8,128)(2,1)} async-done(((bf16[384,1152]{1,0:T(8,128)(2,1)}), bf16[384,1152]{1,0:T(8,128)(2,1)}) %all-reduce.5.cloned.1.call-update) | async-done | bytes 884752 | tf_op jit(solution)/shard_map/psum | solution.py:397
  190.5 5.0 %fusion.86.grad_ref = f32[768,538]{1,0:T(8,128)} fusion(bf16[768,1152]{1,0:T(8,128)(2,1)S(1)} %fusion.85, bf16[1152,538]{1,0:T(8,128)(2,1)} %all-gather.11.cloned.1.call-done), kind=kOutput, calls=%fused_computation.192 | convolution fusion | flops 951975936 | bytes 4661760 | tf_op jit(solution)/shard_map/dot_general | solution.py:22
  195.4 26.0 %all-gather.13.cloned.1.call-done.up_ref = bf16[1152,538]{1,0:T(8,128)(2,1)} async-done(((bf16[288,538]{1,0:T(8,128)(2,1)}), bf16[1152,538]{1,0:T(8,128)(2,1)}) %all-gather.13.cloned.1.call-update) | async-done | bytes 1239568 | tf_op jit(solution)/shard_map/all_gather | solution.py:370
  221.5 9.2 %mlp.1 = (bf16[768,538]{1,0:T(8,128)(2,1)}, bf16[768,538]{1,0:T(8,128)(2,1)}, bf16[768,1152]{1,0:T(8,128)(2,1)}, f32[1,538]{1,0:T(1,128)}) custom-call(s32[1]{0:T(128)} %bitcast.6.core_ref, bf16[768,1152]{1,0:T(8,128)(2,1)} %bitcast.126, bf16[1152,538]{1,0:T(8,128)(2,1)} %all-gather.13.cloned.1.call-done.up_ref, f32[1,538]{1,0:T(1,128)} %broadcast_in_dim.21.bias_ref, ...), custom_call_target="tpu_custom_call" | custom-call | tf_op jit(solution)/shard_map/mlp/pallas_call | solution.py:161
  235.7 46.8 %all-reduce.7.cloned.1.call-done = bf16[384,1152]{1,0:T(8,128)(2,1)} async-done(((bf16[384,1152]{1,0:T(8,128)(2,1)}), bf16[384,1152]{1,0:T(8,128)(2,1)}) %all-reduce.7.cloned.1.call-update) | async-done | bytes 884752 | tf_op jit(solution)/shard_map/psum | solution.py:416
  293.3 10.5 %attend_back.1 = (bf16[432,768]{1,0:T(8,128)(2,1)}, f32[432,1]{1,0:T(8,128)}, bf16[1152,432]{1,0:T(8,128)(2,1)}, bf16[1152,144]{1,0:T(8,128)(2,1)}) custom-call(bf16[768,1152]{1,0:T(8,128)(2,1)} %bitcast.114, bf16[1152,144]{1,0:T(8,128)(2,1)} %bitcast.129, bf16[2,3,72,768]{3,2,1,0:T(8,128)(2,1)} %get-tuple-element.39.qkv_ref, ...), custom_call_target="tpu_custom_call" | custom-call | tf_op jit(solution)/shard_map/attend_back/pallas_call | solution.py:214
  303.9 4.0 fusion.88
  311.1 4.5 fusion.87.w_ref
  315.6 4.4 fusion.89
  320.7 5.7 %first_back.1 = (bf16[4,160,768]{2,1,0:T(8,128)(2,1)}, bf16[4,160,768]{2,1,0:T(8,128)(2,1)}, f32[1152,2]{1,0:T(8,128)}) custom-call(s32[1]{0:T(128)} %bitcast.6.core_ref, bf16[1152,432]{1,0:T(8,128)(2,1)} %fusion.87.w_ref, bf16[432,768]{1,0:T(8,128)(2,1)} %get-tuple-element.41.grad_ref, bf16[1152,768]{1,0:T(8,128)(2,1)} %bitcast.125, ...), custom_call_target="tpu_custom_call" | custom-call | tf_op jit(solution)/shard_map/first_back/pallas_call | solution.py:259
  333.5 7.7 %fusion.33 = f32[1152,768]{1,0:T(8,128)} fusion(bf16[768,538]{1,0:T(8,128)(2,1)S(1)} %copy-done.52, bf16[1152,1152]{1,0:T(8,128)(2,1)} %fusion.12, bf16[1152,538]{1,0:T(8,128)(2,1)} %all-gather.11.cloned.1.call-done), kind=kOutput, calls=%fused_computation.69 | convolution fusion | flops 2379939840 | bytes 8259072 | tf_op jit(solution)/shard_map/dot_general | solution.py:22
  342.4 5.3 %fusion.16 = f32[1152,768]{1,0:T(8,128)} fusion(f32[1152,768]{1,0:T(8,128)} %fusion.33, s32[]{:T(128)S(6)} %select_n.87, bf16[1152,1152]{1,0:T(8,128)(2,1)} %fusion.12, f32[384,1152]{1,0:T(8,128)S(1)} %get-tuple-element.163, pred[1152]{0:T(1024)(128)(4,1)S(1)} %fusion.62), kind=kOutput, calls=%fused_computation.32 | convolution fusion | flops 1020542976 | bytes 7963780 | tf_op jit(solution)/shard_map/dot_general | solution.py:22
  347.7 3.8 all-to-all-start.5
  359.1 12.5 %collective-permute-done.6 = f32[13520]{0:T(1024)S(1)} collective-permute-done((f32[13520]{0:T(1024)S(1)}, f32[13520]{0:T(1024)S(1)}, u32[]{:S(2)}, u32[]{:S(2)}) %collective-permute-start.6) | collective-permute-done | bytes 54112 | tf_op jit(solution)/shard_map/ppermute | solution.py:69
  384.4 17.8 %reduce-scatter.11.cloned.1.call-done = bf16[288,538]{1,0:T(8,128)(2,1)} async-done(((bf16[1152,538]{1,0:T(8,128)(2,1)}), bf16[288,538]{1,0:T(8,128)(2,1)}) %reduce-scatter.11.cloned.1.call-update) | async-done | bytes 309904 | tf_op jit(solution)/shard_map/reduce_scatter | solution.py:344
  405.4 4.8 all-to-all-start.7
  420.1 7.5 %all-to-all-done.7 = bf16[4,72,1076]{2,1,0:T(8,128)(2,1)S(1)} async-done(((bf16[4,72,1076]{2,1,0:T(8,128)(2,1)}), bf16[4,72,1076]{2,1,0:T(8,128)(2,1)S(1)}, u32[]{:S(2)}, u32[]{:S(2)}) %all-to-all-start.7) | async-done | bytes 619808 | tf_op jit(solution)/shard_map/all_to_all | solution.py:58
  427.6 3.5 all-to-all-start.4
  436.3 6.4 %multiply_subtract_fusion.1 = (f32[72,1,2152]{2,1,0:T(1,128)}, f32[72,1,2152]{2,1,0:T(1,128)}, f32[72,1,2152]{2,1,0:T(1,128)}) fusion(f32[72,1,2152]{2,1,0:T(1,128)S(1)} %copy-done.10, f32[72,1,2152]{2,1,0:T(1,128)S(1)} %broadcast_in_dim_reshape.8, f32[72,1,2152]{2,1,0:T(1,128)} %param.28, f32[72,1,2152]{2,1,0:T(1,128)} %param.32), kind=kLoop, calls=%fused_computation.83 | loop fusion | flops 2324160 | bytes 4338432 | tf_op jit(solution)/shard_map/sub | solution.py:279
  442.8 12.2 %all-to-all-done.4 = bf16[4,160,768]{2,1,0:T(8,128)(2,1)S(1)} async-done(((bf16[4,160,768]{2,1,0:T(8,128)(2,1)}), bf16[4,160,768]{2,1,0:T(8,128)(2,1)S(1)}, u32[]{:S(2)}, u32[]{:S(2)}) %all-to-all-start.4) | async-done | bytes 983072 | tf_op jit(solution)/shard_map/all_to_all | solution.py:58
  455.0 3.8 all-to-all-start.3
  458.8 5.9 %multiply_subtract_fusion = (f32[2152,72,1]{0,2,1:T(1,128)}, f32[2152,72,1]{0,2,1:T(1,128)}, f32[2152,72,1]{0,2,1:T(1,128)}) fusion(f32[2152,72,1]{0,2,1:T(1,128)S(1)} %copy-done.12, f32[2152,72,1]{0,1,2:T(8,128)S(1)} %copy-done.13, f32[2152,72]{0,1:T(8,128)} %multiply_multiply_fusion, f32[2152,72,1]{0,2,1:T(1,128)} %param.33), kind=kLoop, calls=%fused_computation.81 | loop fusion | flops 1549440 | bytes 4338432 | tf_op jit(solution)/shard_map/sub | solution.py:279
  466.6 13.8 %all-to-all-done.3 = bf16[4,144,768]{2,1,0:T(8,128)(2,1)S(1)} async-done(((bf16[4,144,768]{2,1,0:T(8,128)(2,1)}), bf16[4,144,768]{2,1,0:T(8,128)(2,1)S(1)}, u32[]{:S(2)}, u32[]{:S(2)}) %all-to-all-start.3) | async-done | bytes 884768 | tf_op jit(solution)/shard_map/all_to_all | solution.py:58
  (322 shorter events, 118.6 us)
Async XLA Ops:
  11.7 44.7 %all-to-all-start.1 = ((bf16[4,72,432]{2,1,0:T(8,128)(2,1)}), bf16[4,72,432]{2,1,0:T(8,128)(2,1)}, u32[]{:S(2)}, u32[]{:S(2)}) async-start(bf16[4,72,432]{2,1,0:T(8,128)(2,1)} %copy.119), calls=%async_computation.1 | async-start | bytes 589824 | tf_op jit(solution)/shard_map/all_to_all | solution.py:58
  20.0 28.2 %copy-start.39 = (f32[2,1152]{1,0:T(2,128)S(1)}, f32[2,1152]{1,0:T(2,128)}, u32[]{:S(2)}) copy-start(f32[2,1152]{1,0:T(2,128)} %param.34) | copy-start | bytes 27652
  20.0 29.2 %copy-start.11 = (f32[2152,72,1]{0,2,1:T(1,128)S(1)}, f32[2152,72,1]{0,2,1:T(1,128)}, u32[]{:S(2)}) copy-start(f32[2152,72,1]{0,2,1:T(1,128)} %param.25) | copy-start | bytes 1859332
  56.4 23.1 %all-to-all-start = ((bf16[4,72,1220]{2,1,0:T(8,128)(2,1)}), bf16[4,72,1220]{2,1,0:T(8,128)(2,1)S(1)}, u32[]{:S(2)}, u32[]{:S(2)}) async-start(bf16[4,72,1220]{2,1,0:T(8,128)(2,1)} %concatenate.22), calls=%async_computation | async-start | bytes 1474560 | tf_op jit(solution)/shard_map/all_to_all | solution.py:58
  62.9 64.4 %copy-start.1 = (bf16[2,576,768]{2,1,0:T(8,128)(2,1)}, bf16[2,576,768]{2,1,0:T(8,128)(2,1)S(1)}, u32[]{:S(2)}) copy-start(bf16[2,576,768]{2,1,0:T(8,128)(2,1)S(1)} %pad_maximum_fusion) | copy-start | bytes 5308420
  62.9 22.6 %copy-start.31 = (f32[768]{0:T(1024)}, f32[768]{0:T(1024)S(1)}, u32[]{:S(2)}) copy-start(f32[768]{0:T(1024)S(1)} %broadcast_multiply_fusion) | copy-start | bytes 9220
  63.4 22.1 %copy-start.37 = (f32[768]{0:T(1024)}, f32[768]{0:T(1024)S(1)}, u32[]{:S(2)}) copy-start(f32[768]{0:T(1024)S(1)} %add_rsqrt_fusion) | copy-start | bytes 9220
  81.8 25.2 %all-to-all-start.2 = ((bf16[4,288,432]{2,1,0:T(8,128)(2,1)}), bf16[4,288,432]{2,1,0:T(8,128)(2,1)S(1)}, u32[]{:S(2)}, u32[]{:S(2)}) async-start(bf16[4,288,432]{2,1,0:T(8,128)(2,1)} %broadcast_in_dim.16), calls=%async_computation.2 | async-start | bytes 2359296 | tf_op jit(solution)/shard_map/all_to_all | solution.py:49
  85.5 90.6 %all-reduce.5.cloned.1.call-start = ((), (), s32[]{:S(2)}) async-start(), calls=%async_computation.13 | async-start | bytes 1769472 | tf_op jit(solution)/shard_map/psum | solution.py:397
  116.4 2.6 collective-permute-start
  121.4 64.0 %all-gather.15.cloned.1.call-start = ((), (), s32[]{:S(2)}) async-start(), calls=%async_computation.15 | async-start | bytes 1990656 | tf_op jit(solution)/shard_map/all_gather | solution.py:372
  122.2 68.3 %all-gather.11.cloned.1.call-start = ((), (), s32[]{:S(2)}) async-start(), calls=%async_computation.12 | async-start | bytes 1843200 | tf_op jit(solution)/shard_map/all_gather | solution.py:371
  123.5 97.9 %all-gather.13.cloned.1.call-start = ((), (), s32[]{:S(2)}) async-start(), calls=%async_computation.14 | async-start | bytes 1843200 | tf_op jit(solution)/shard_map/all_gather | solution.py:370
  130.5 152.1 %all-reduce.7.cloned.1.call-start = ((), (), s32[]{:S(2)}) async-start(), calls=%async_computation.16 | async-start | bytes 1769472 | tf_op jit(solution)/shard_map/psum | solution.py:416
  190.4 94.8 %copy-start.24 = (bf16[768,1152]{1,0:T(8,128)(2,1)}, bf16[768,1152]{1,0:T(8,128)(2,1)S(1)}, u32[]{:S(2)}) copy-start(bf16[768,1152]{1,0:T(8,128)(2,1)S(1)} %fusion.85) | copy-start | bytes 5308420
  232.0 2.5 collective-permute-start.1
  235.7 143.3 %reduce-scatter.7.cloned.1.call-start = ((), (), s32[]{:S(2)}) async-start(), calls=%async_computation.18 | async-start | bytes 737280 | tf_op jit(solution)/shard_map/reduce_scatter | solution.py:344
  303.9 80.5 %reduce-scatter.9.cloned.1.call-start = ((), (), s32[]{:S(2)}) async-start(), calls=%async_computation.19 | async-start | bytes 1843200 | tf_op jit(solution)/shard_map/reduce_scatter | solution.py:344
  307.9 94.2 %reduce-scatter.11.cloned.1.call-start = ((), (), s32[]{:S(2)}) async-start(), calls=%async_computation.20 | async-start | bytes 1843200 | tf_op jit(solution)/shard_map/reduce_scatter | solution.py:344
  330.9 1.3 collective-permute-start.3
  332.2 9.0 %collective-permute-start.4 = (f32[13520]{0:T(1024)S(1)}, f32[13520]{0:T(1024)S(1)}, u32[]{:S(2)}, u32[]{:S(2)}) collective-permute-start(f32[13520]{0:T(1024)S(1)} %add.394), channel_id=1, source_target_pairs={{0,2},{2,0},{4,6},{6,4},{1,3},{3,1},{5,7},{7,5},{8,10},{10,8},{12,... | collective-permute-start | bytes 162248 | tf_op jit(solution)/shard_map/ppermute | solution.py:69
  341.3 10.2 %collective-permute-start.5 = (f32[13520]{0:T(1024)S(1)}, f32[13520]{0:T(1024)S(1)}, u32[]{:S(2)}, u32[]{:S(2)}) collective-permute-start(f32[13520]{0:T(1024)S(1)} %add.395), channel_id=1, source_target_pairs={{0,4},{2,6},{4,0},{6,2},{1,5},{3,7},{5,1},{7,3},{8,12},{10,14},{12... | collective-permute-start | bytes 162248 | tf_op jit(solution)/shard_map/ppermute | solution.py:69
  347.7 30.9 %all-to-all-start.5 = ((bf16[4,288,432]{2,1,0:T(8,128)(2,1)}), bf16[4,288,432]{2,1,0:T(8,128)(2,1)S(1)}, u32[]{:S(2)}, u32[]{:S(2)}) async-start(bf16[4,288,432]{2,1,0:T(8,128)(2,1)} %bitcast.141), calls=%async_computation.7 | async-start | bytes 2359296 | tf_op jit(solution)/shard_map/all_to_all | solution.py:431
  351.5 103.4 %reduce-scatter.5.cloned.1.call-start = ((), (), s32[]{:S(2)}) async-start(), calls=%async_computation.17 | async-start | bytes 2654208 | tf_op jit(solution)/shard_map/reduce_scatter | solution.py:453
  351.5 20.0 %collective-permute-start.6 = (f32[13520]{0:T(1024)S(1)}, f32[13520]{0:T(1024)S(1)}, u32[]{:S(2)}, u32[]{:S(2)}) collective-permute-start(f32[13520]{0:T(1024)S(1)} %add.396), channel_id=1, source_target_pairs={{0,8},{8,0},{16,24},{24,16},{1,9},{9,1},{17,25},{25,17},{2,10},{10... | collective-permute-start | bytes 162248 | tf_op jit(solution)/shard_map/ppermute | solution.py:69
  357.7 46.5 %collective-permute-start.2 = (bf16[4,160,768]{2,1,0:T(8,128)(2,1)}, bf16[4,160,768]{2,1,0:T(8,128)(2,1)S(1)}, u32[]{:S(2)}, u32[]{:S(2)}) collective-permute-start(bf16[4,160,768]{2,1,0:T(8,128)(2,1)} %get-tuple-element.43), channel_id=1, source_target_pairs={{0,1},{1,0},{2,3},{3,2},{4,5},{5,4},{6,7},{7,6},{8,9},{9,8},{10,11... | collective-permute-start | bytes 2949128 | tf_op jit(solution)/shard_map/ppermute | solution.py:37
  371.5 5.1 %collective-permute-start.7 = (f32[13520]{0:T(1024)S(1)}, f32[13520]{0:T(1024)S(1)}, u32[]{:S(2)}, u32[]{:S(2)}) collective-permute-start(f32[13520]{0:T(1024)S(1)} %add.397), channel_id=1, source_target_pairs={{0,16},{8,24},{16,0},{24,8},{1,17},{9,25},{17,1},{25,9},{2,18},{10... | collective-permute-start | bytes 162248 | tf_op jit(solution)/shard_map/ppermute | solution.py:69
  378.9 25.3 %copy-start.18 = (bf16[4,160,768]{2,1,0:T(8,128)(2,1)S(1)}, bf16[4,160,768]{2,1,0:T(8,128)(2,1)}, u32[]{:S(2)}) copy-start(bf16[4,160,768]{2,1,0:T(8,128)(2,1)} %get-tuple-element.42) | copy-start | bytes 2949124
  380.9 24.6 %all-to-all-start.6 = ((bf16[4,72,576]{2,1,0:T(8,128)(2,1)}), bf16[4,72,576]{2,1,0:T(8,128)(2,1)S(1)}, u32[]{:S(2)}, u32[]{:S(2)}) async-start(bf16[4,72,576]{2,1,0:T(8,128)(2,1)} %bitcast.37), calls=%async_computation.8 | async-start | bytes 737280 | tf_op jit(solution)/shard_map/all_to_all | solution.py:58
  405.4 22.2 %all-to-all-start.7 = ((bf16[4,72,1076]{2,1,0:T(8,128)(2,1)}), bf16[4,72,1076]{2,1,0:T(8,128)(2,1)S(1)}, u32[]{:S(2)}, u32[]{:S(2)}) async-start(bf16[4,72,1076]{2,1,0:T(8,128)(2,1)} %bitcast.43), calls=%async_computation.11 | async-start | bytes 1327104 | tf_op jit(solution)/shard_map/all_to_all | solution.py:58
  427.6 27.3 %all-to-all-start.4 = ((bf16[4,160,768]{2,1,0:T(8,128)(2,1)}), bf16[4,160,768]{2,1,0:T(8,128)(2,1)S(1)}, u32[]{:S(2)}, u32[]{:S(2)}) async-start(bf16[4,160,768]{2,1,0:T(8,128)(2,1)} %add_convert_fusion.2), calls=%async_computation.5 | async-start | bytes 1966080 | tf_op jit(solution)/shard_map/all_to_all | solution.py:58
  455.0 25.5 %all-to-all-start.3 = ((bf16[4,144,768]{2,1,0:T(8,128)(2,1)}), bf16[4,144,768]{2,1,0:T(8,128)(2,1)S(1)}, u32[]{:S(2)}, u32[]{:S(2)}) async-start(bf16[4,144,768]{2,1,0:T(8,128)(2,1)} %bitcast.143), calls=%async_computation.4 | async-start | bytes 1769472 | tf_op jit(solution)/shard_map/all_to_all | solution.py:58
  (46 other events, 184.8 us)
Sparse Core Ops, SparseCore 0:
  121.5 54.4 all-reduce.4
  235.8 46.7 all-reduce.6
Sparse Core Ops, SparseCore 1:
  124.1 33.0 all-gather.14
  159.5 29.6 all-gather.10
  191.4 30.0 all-gather.12
  303.9 24.3 reduce-scatter.6
  331.6 38.3 reduce-scatter.8
  373.0 29.1 reduce-scatter.10
  404.4 9.1 reduce-scatter.4
where the time goes:
time: 499 us; the launch traced here: 489 us
  waiting for transfers between devices  204 us (41%)
  other arithmetic  54.7 us (11%)
  blocking collectives  51.1 us (10%)
  matrix products  45.1 us (9%)
  local copies, waits for them, and re-layouts  42.7 us (9%)
  starting transfers between devices  39.6 us (8%)
  Pallas kernels  33.8 us (7%)
  between operations  18.5 us (4%)
    all_to_all x6, waiting for transfers between devices, exchange_rows(): return lax.all_to_all(blocks, 'row', 0, 0)  49.5 us
    psum x1, waiting for transfers between devices, shards(): two_grad = lax.psum(pair.astype(LOW), 'row').astype(jnp.float32)  46.8 us
    psum x1, waiting for transfers between devices, shards(): branch = lax.psum(pair, 'row').astype(jnp.float32)  45.5 us
    dot_general x10, matrix products, dot(): lax.dot_general(left, right, (((left_dim,), (right_dim,)), ((), ())), pre...  45.1 us
    all_gather x1, waiting for transfers between devices, shards(): lax.all_gather(rest[:, width:width + hidden_width], 'dp', axis=0, tiled=T...  26 us
    all_to_all x6, starting transfers between devices, exchange_rows(): return lax.all_to_all(blocks, 'row', 0, 0)  25.5 us
    all_gather x1, blocking collectives, shards(): x_all = both_cores(lax.all_gather(x_own, 'row', axis=0, tiled=True))  22.4 us
    reduce_scatter x3, waiting for transfers between devices, scattered(): return lax.psum_scatter(gradient, 'dp', scatter_dimension=0, tiled=True)  17.8 us
  transfers between devices with their start and end apart: 25, of which 12 were waited for; matrix products, arithmetic and copies ran while one was open for 25% of the time, Pallas kernels for 1%

commit v1 on v0

--- a/solution.py
+++ b/solution.py
@@ -56,6 +56,30 @@
 
 def exchange_rows(blocks):
     return lax.all_to_all(blocks, "row", 0, 0)
+
+
+def sum_blocks(blocks, axis):
+    size = lax.axis_size(axis)
+    if size > 4:
+        return jnp.sum(lax.all_to_all(blocks, axis, 0, 0).astype(jnp.float32), axis=0)
+    me = lax.axis_index(axis)
+    got = [
+        lax.ppermute(
+            lax.dynamic_index_in_dim(blocks, me ^ step, 0, keepdims=False),
+            axis,
+            [(i, i ^ step) for i in range(size)],
+        )
+        for step in range(1, size)
+    ]
+    total = lax.dynamic_index_in_dim(blocks, me, 0, keepdims=False).astype(jnp.float32)
+    for block in got:
+        total = total + block.astype(jnp.float32)
+    return total
+
+
+def sum_over_rows(half):
+    summed = lax.psum_scatter(half.astype(LOW), "row", scatter_dimension=0, tiled=True)
+    return summed.astype(jnp.float32)
 
 
 def all_sum(vector):
@@ -312,18 +336,18 @@
     heads = width // HEAD
     hidden_width = FF // group
     own = core * n_row + row
-    padded = -(-tokens // (group * 16)) * (group * 16)
+    chunk = -(-tokens // (group * 16)) * 16
+    padded = chunk * group
     half = padded // n_col
     shard_rows = qkv_master.shape[0]
 
-    place = lax.broadcasted_iota(jnp.int32, (D, D), 0)
-    source = lax.broadcasted_iota(jnp.int32, (D, D), 1)
+    place = jnp.arange(D)
     feature = (
         ((place // width) % n_row) * n_col + place // (width * n_row)
     ) * width + place % width
-    order = lax.optimization_barrier(
-        (source == (feature % n_dp) * (D // n_dp) + feature // n_dp).astype(LOW)
-    )
+    place = (feature % n_dp) * (D // n_dp) + feature // n_dp
+    order = (lax.broadcasted_iota(jnp.int32, (D, D), 1) == place[:, None]).astype(LOW)
+    order = lax.optimization_barrier(order)
 
     def mixed(vector):
         return vector.reshape(n_row, n_col, width).transpose(1, 0, 2).reshape(D)
@@ -341,7 +365,7 @@
         return rows.reshape(shard_rows, parts, -1).transpose(1, 0, 2)
 
     def scattered(gradient):
-        return lax.psum_scatter(gradient, "dp", scatter_dimension=0, tiled=True)
+        return sum_blocks(gradient.reshape(n_dp, D // n_dp, -1), "dp").astype(LOW)
 
     def returned(rows):
         blocks = exchange_rows(rows.reshape(n_row, shard_rows, -1))
@@ -353,23 +377,33 @@
     def long(array):
         return jnp.pad(array, ((0, 0), (0, padded - tokens)))
 
-    qkv_rows = exchange_rows(to_owner(qkv_master[:, 0].astype(LOW), n_row))
+    first_rows = jnp.concatenate(
+        [
+            to_owner(qkv_master[:, 0].astype(LOW), n_row),
+            to_owner(out_master[:, :, 0].T.astype(LOW), n_row),
+        ],
+        axis=2,
+    )
+    first_rows = exchange_rows(first_rows).reshape(D // n_dp, -1)
     x_own = long(inputs.T)
-    x_all = both_cores(lax.all_gather(x_own, "row", axis=0, tiled=True))
-    w_qkv = send_copies(qkv_rows.reshape(D // n_dp, -1), "dp")
+    x_rows = lax.all_gather(x_own, "row", axis=0, tiled=True)
+    x_all = both_cores(x_rows)
+    w_first = send_copies(first_rows, "dp")
+    w_qkv = w_first[:, : 3 * width]
+    w_out = w_first[:, 3 * width :]
     rest = jnp.concatenate(
         [
-            to_owner(out_master[:, :, 0].T.astype(LOW), n_row),
             to_owner(up_master[:, 0].astype(LOW), n_row),
             to_owner(down_master[:, :, 0].T.astype(LOW), n_row),
         ],
         axis=2,
     )
-    rest = exchange_rows(rest).reshape(D // n_dp, -1)
-    w_out = lax.all_gather(rest[:, :width], "dp", axis=0, tiled=True)
-    w_up = lax.all_gather(rest[:, width : width + hidden_width], "dp", axis=0, tiled=True)
-    w_down = lax.all_gather(rest[:, width + hidden_width :], "dp", axis=0, tiled=True)
-    cot_all = lax.all_gather(long(cotangent.T), ("row", "col"), axis=0, tiled=True)
+    rest = exchange_rows(rest + zero_of(w_first).astype(LOW)).reshape(D // n_dp, -1)
+    w_rest = send_copies(rest, "dp")
+    w_up = w_rest[:, :hidden_width]
+    w_down = w_rest[:, hidden_width:]
+    cot_own = long(cotangent.T) + zero_of(x_rows).astype(LOW)
+    cot_all = lax.all_gather(cot_own, ("row", "col"), axis=0, tiled=True)
 
     gain_one = mixed(norm_gains[0])
     gain_two = dealt(norm_gains[1])
@@ -393,45 +427,59 @@
     za = dot(order, za, 0, 0, LOW)
 
     qkv, attended, theirs, mine = attend(core_of, w_qkv, za, qkv_bias, w_out)
-    pair = (mine.astype(jnp.float32) + swap_cores(theirs).astype(jnp.float32)).astype(LOW)
-    branch = lax.psum(pair, "row").astype(jnp.float32)
-
-    x_half = lax.dynamic_slice_in_dim(x_all, core * half, half, axis=1)
-    x_half = dot(x_half, order, 0, 0)
+    branch = sum_over_rows(mine.astype(jnp.float32) + swap_cores(theirs).astype(jnp.float32))
+
+    pick = lax.broadcasted_iota(jnp.int32, (chunk, padded), 0) + own * chunk
+    pick = (lax.broadcasted_iota(jnp.int32, (chunk, padded), 1) == pick).astype(LOW)
+    x_mine = dot(dot(pick, x_all, 1, 1, LOW), order, 1, 0)
     cot_mixed = cot_all.reshape(n_row, n_col, width, padded).transpose(1, 0, 2, 3)
     cot_tokens = dot(cot_mixed.reshape(D, padded), order, 0, 0, LOW)
     active_grad = dot(cot_tokens, w_down, 1, 0)
-    cot_half = take(cot_tokens, core, half).astype(jnp.float32)
+    cot_mine = take(cot_tokens, own, chunk).astype(jnp.float32)
     qkv_mixed = dot(order, w_qkv, 1, 0, LOW)
     down_mixed = dot(order, w_down, 1, 0, LOW)
 
-    middle = x_half + branch + out_bias[None, :]
+    middle = x_mine + branch + out_bias[None, :]
     center = middle - jnp.sum(middle, axis=1, keepdims=True) / D
     inverse_two = lax.rsqrt(jnp.sum(center * center, axis=1, keepdims=True) / D + NORM_EPS)
     normed_two = center * inverse_two
-    zb = both_cores((normed_two * gain_two + shift_two).astype(LOW))
+    zb = (normed_two * gain_two + shift_two).astype(LOW)
+    zb = both_cores(lax.all_gather(zb, "row", axis=0, tiled=True))
 
     active, hidden_grad, two_parts, up_sums = mlp(core_of, zb, w_up, up_bias[None, :], active_grad)
-    pair = two_parts[half:].astype(jnp.float32) + swap_cores(two_parts[:half]).astype(jnp.float32)
-    two_grad = lax.psum(pair.astype(LOW), "row").astype(jnp.float32)
-    down_rows = scattered(dot(cot_tokens, active, 0, 0, LOW))
-    up_rows = scattered(dot(zb, hidden_grad, 0, 0, LOW))
+    two_grad = sum_over_rows(
+        two_parts[half:].astype(jnp.float32) + swap_cores(two_parts[:half]).astype(jnp.float32)
+    )
+
+    middle_mixed = dot(order, middle.astype(LOW), 1, 1, LOW)
+    result = dot(down_mixed, active, 1, 1) + dot(middle_mixed, pick, 1, 0)
+    result = result.astype(LOW).reshape(n_col, D // n_col, padded)
+    theirs = lax.dynamic_index_in_dim(result, 1 - core, 0, keepdims=False)
+    mine = lax.dynamic_index_in_dim(result, core, 0, keepdims=False)
+    result = mine.astype(jnp.float32) + swap_cores(theirs).astype(jnp.float32)
+    rest_grad = jnp.concatenate(
+        [dot(zb, hidden_grad, 0, 0, LOW), dot(cot_tokens, active, 0, 0, LOW)], axis=1
+    )
+    rest_rows = scattered(rest_grad)
 
     scaled = two_grad * gain_two
     first_sum = jnp.sum(scaled, axis=1, keepdims=True) / D
     second_sum = jnp.sum(scaled * normed_two, axis=1, keepdims=True) / D
-    middle_grad = cot_half + inverse_two * (scaled - first_sum - normed_two * second_sum)
+    middle_grad = cot_mine + inverse_two * (scaled - first_sum - normed_two * second_sum)
     middle_grad = middle_grad.astype(LOW)
-    branch_all = both_cores(middle_grad)
+    branch_all = both_cores(lax.all_gather(middle_grad, "row", axis=0, tiled=True))
+
+    result = (result + zero_of(branch_all)).astype(LOW).reshape(n_row, width, padded)
+    result = sum_blocks(result, "row") + down_bias[:, None]
+    result = result.astype(LOW)[:, :tokens].T
 
     qkv_grad, bias_sums, qkv_full, out_full = attend_back(branch_all, w_out, qkv, za, attended)
     theirs, mine, one_sums = first_back(
         core_of, qkv_mixed, qkv_grad, x_all, x_mean, inverse_one, gain_one[:, None], width, n_row
     )
-    qkv_blocks = lax.all_to_all(qkv_full.reshape(n_dp, D // n_dp, -1), "dp", 0, 0)
-    qkv_rows = jnp.sum(qkv_blocks.astype(jnp.float32), axis=0).astype(LOW)
-    pair = (mine.astype(jnp.float32) + swap_cores(theirs).astype(jnp.float32)).astype(LOW)
-    one_grad = jnp.sum(exchange_rows(pair).astype(jnp.float32), axis=0)
+    first_rows = scattered(jnp.concatenate([qkv_full, out_full], axis=1))
+    pair = mine.astype(jnp.float32) + swap_cores(theirs).astype(jnp.float32)
+    one_grad = sum_over_rows(pair.reshape(-1, padded))
     own_gain = lax.dynamic_slice_in_dim(norm_gains[0], feature_start, width)[:, None]
     own_normed = (x_own.astype(jnp.float32) - x_mean) * inverse_one
     own_order = lax.dynamic_slice_in_dim(order, own * width, width, axis=0)
@@ -443,34 +491,20 @@
     )
     input_grad = input_grad.astype(LOW)[:, :tokens].T
 
-    middle_mixed = dot(order, middle.astype(LOW), 1, 1)
-    at_row = ((jnp.arange(D) // width) % n_row == row)[:, None]
-    middle_mixed = jnp.where(at_row, middle_mixed, 0.0)
-    middle_mixed = lax.dynamic_update_slice_in_dim(
-        jnp.zeros((D, padded), jnp.float32), middle_mixed, core * half, 1
-    )
-    result = (dot(down_mixed, active, 1, 1) + middle_mixed + zero_of(branch_all)).astype(LOW)
-    result = lax.psum_scatter(result, "col", scatter_dimension=0, tiled=True)
-    result = exchange_rows(result.reshape(n_row, width, padded))
-    result = jnp.sum(result.astype(jnp.float32), axis=0) + down_bias[:, None]
-    result = result.astype(LOW)[:, :tokens].T
-
-    out_rows = scattered(out_full)
-    last = returned(jnp.concatenate([out_rows, qkv_rows], axis=1))
-    out_blocks = last[:, :, :width]
-    qkv_blocks = last[:, :, width:]
+    last = returned(first_rows)
+    qkv_blocks = last[:, :, : 3 * width]
+    out_blocks = last[:, :, 3 * width :]
 
     bias_sums = bias_sums.reshape(heads, 3, HEAD)
-    once = (row == 0).astype(jnp.float32)
     shared = jnp.stack(
         [
             jnp.sum(two_grad * normed_two, axis=0),
             jnp.sum(two_grad, axis=0),
             jnp.sum(middle_grad, axis=0, dtype=jnp.float32),
-            jnp.sum(cot_half, axis=0),
+            jnp.sum(cot_mine, axis=0),
         ]
     )
-    shared = (shared * once).reshape(4, n_dp, D // n_dp).transpose(0, 2, 1).reshape(4, D)
+    shared = shared.reshape(4, n_dp, D // n_dp).transpose(0, 2, 1).reshape(4, D)
     bias_grad = jnp.concatenate(
         [
             plain(one_sums[:, 0]),
@@ -494,7 +528,7 @@
     bias_total = total[2 * D :]
 
     later = zero_of(qkv_grad)
-    first = returned(jnp.concatenate([up_rows, down_rows], axis=1))
+    first = returned(rest_rows)
     up_blocks = first[:, :, :hidden_width]
     down_blocks = first[:, :, hidden_width:]
     q_new = adam_update(

time: 499 us -> 455 us (0.912)
  waiting for transfers between devices: 204 us -> 75.6 us
  local copies, waits for them, and re-layouts: 42.7 us -> 107 us
  blocking collectives: 51.1 us -> 78.6 us
  matrix products: 45.1 us -> 37.3 us
    psum x2 -> x0, waiting for transfers between devices: 92.3 us -> none  [the longest x1 46.8 us: shards(): two_grad = lax.psum(pair.astype(LOW), 'row').astype(jnp.float32)]
    all_to_all x6 -> x4, waiting for transfers between devices: 49.5 us -> 10.5 us  [exchange_rows(): return lax.all_to_all(blocks, 'row', 0, 0)]
    all_gather x2 -> x3, blocking collectives: 35.9 us -> 63.7 us  [the longest x1 25.8 us: shards(): x_rows = lax.all_gather(x_own, 'row', axis=0, tiled=True)]
    all_gather x3 -> x1, waiting for transfers between devices: 26.1 us -> 0.02 us  [shards(): cot_all = lax.all_gather(cot_own, ('row', 'col'), axis=0, tiled=True)]
    ppermute x0 -> x9, waiting for transfers between devices: none -> 23.2 us  [sum_blocks(): lax.ppermute(lax.dynamic_index_in_dim(blocks, me ^ step, 0, keepdims=Fals...]
    unnamed x123 -> x121, local copies, waits for them, and re-layouts: 11.6 us -> 29.2 us
    all_to_all x1 -> x2, waiting for transfers between devices: 0.01 us -> 12.1 us  [send_copies(): return lax.all_to_all(copies, axis, 0, 0).reshape(-1, block.shape[1])]
    ppermute x0 -> x9, starting transfers between devices: none -> 11.5 us  [sum_blocks(): lax.ppermute(lax.dynamic_index_in_dim(blocks, me ^ step, 0, keepdims=Fals...]
  transfers between devices with their start and end apart: 25 -> 28, of which waited for: 12 -> 12; matrix products, arithmetic and copies ran while one was open for 25% -> 39% of each run, Pallas kernels for 1% -> 6%
where the time goes in v1:
time: 455 us; the launch traced here: 448 us
  local copies, waits for them, and re-layouts  107 us (24%)
  blocking collectives  78.6 us (17%)
  waiting for transfers between devices  75.6 us (17%)
  other arithmetic  52.7 us (12%)
  starting transfers between devices  42.8 us (9%)
  matrix products  37.3 us (8%)
  Pallas kernels  33.9 us (7%)
  between operations  19.6 us (4%)
    dot_general x10, matrix products, dot(): lax.dot_general(left, right, (((left_dim,), (right_dim,)), ((), ())), pre...  37.3 us
    unnamed x121, local copies, waits for them, and re-layouts  29.2 us
    all_gather x1, blocking collectives, shards(): x_rows = lax.all_gather(x_own, 'row', axis=0, tiled=True)  25.8 us
    ppermute x9, waiting for transfers between devices, sum_blocks(): lax.ppermute(lax.dynamic_index_in_dim(blocks, me ^ step, 0, keepdims=Fals...  23.2 us
    all_gather x1, blocking collectives, shards(): lax.all_gather(middle_grad, 'row', axis=0, tiled=True)  18.9 us
    all_gather x1, blocking collectives, shards(): zb = both_cores(lax.all_gather(zb, 'row', axis=0, tiled=True))  18.9 us
    all_to_all x4, starting transfers between devices, exchange_rows(): return lax.all_to_all(blocks, 'row', 0, 0)  18.5 us
    ppermute x5, waiting for transfers between devices, all_sum(): lax.ppermute(vector, axis, [(i, i ^ step) for i in range(size)])  16.9 us
  transfers between devices with their start and end apart: 28, of which 12 were waited for; matrix products, arithmetic and copies ran while one was open for 39% of the time, Pallas kernels for 6%

profile of v1, /device:TPU:0, one launch (start us, length us, event | category | flops | bytes accessed | tf_op | source)
XLA Modules:
  0.0 447.8 jit_solution(4002056466836834124)
XLA Ops:
  13.1 6.3 %all-to-all-start = ((bf16[4,72,576]{2,1,0:T(8,128)(2,1)}), bf16[4,72,576]{2,1,0:T(8,128)(2,1)}, u32[]{:S(2)}, u32[]{:S(2)}) async-start(bf16[4,72,576]{2,1,0:T(8,128)(2,1)} %copy.146), calls=%async_computation | async-start | bytes 737280 | tf_op jit(solution)/shard_map/all_to_all | solution.py:58
  19.5 25.8 %all_gather.48 = bf16[576,768]{1,0:T(8,128)(2,1)S(1)} all-gather(bf16[144,768]{1,0:T(8,128)(2,1)S(1)} %pad.7), channel_id=1, replica_groups=mesh['dp'=4,'row'=4,'col'=2] {'row'}, dimensions={0}, use_global_device_ids=true | all-gather | bytes 1105920 | tf_op jit(solution)/shard_map/all_gather | solution.py:389
  68.5 4.3 all-to-all-start.1
  75.6 4.0 fusion.4.za_ref
  79.7 12.1 %all-to-all-done.1 = bf16[4,288,576]{2,1,0:T(8,128)(2,1)} async-done(((bf16[4,288,576]{2,1,0:T(8,128)(2,1)}), bf16[4,288,576]{2,1,0:T(8,128)(2,1)}, u32[]{:S(2)}, u32[]{:S(2)}) %all-to-all-start.1) | async-done | bytes 1327136 | tf_op jit(solution)/shard_map/all_to_all | solution.py:49
  96.2 8.5 %attend.1 = (bf16[2,3,72,768]{3,2,1,0:T(8,128)(2,1)}, bf16[768,144]{1,0:T(8,128)(2,1)}, bf16[384,1152]{1,0:T(8,128)(2,1)}, bf16[384,1152]{1,0:T(8,128)(2,1)}) custom-call(s32[1]{0:T(128)} %bitcast.11.core_ref, bf16[1152,432]{1,0:T(8,128)(2,1)} %slice.159.w_ref, bf16[1152,768]{1,0:T(8,128)(2,1)} %fusion.4.za_ref, f32[432,1]{1,0:T(8,128)} %reshape.443.bias_ref, ...), custom_call_target="tpu_custom_call" | custom-call | tf_op jit(solution)/shard_map/attend/pallas_call | solution.py:142
  118.7 4.1 all-to-all-start.2
  140.7 3.4 fusion.20
  148.1 4.6 %all-to-all-start.3 = ((bf16[4,288,1076]{2,1,0:T(8,128)(2,1)}), bf16[4,288,1076]{2,1,0:T(8,128)(2,1)}, u32[]{:S(2)}, u32[]{:S(2)}) async-start(bf16[4,288,1076]{2,1,0:T(8,128)(2,1)} %broadcast_in_dim.11), calls=%async_computation.3 | async-start | bytes 5308416 | tf_op jit(solution)/shard_map/all_to_all | solution.py:49
  154.4 3.8 fusion.108
  160.4 18.9 %all_gather.53 = bf16[384,1152]{1,0:T(8,128)(2,1)S(1)} all-gather(bf16[96,1152]{1,0:T(8,128)(2,1)S(1)} %add_convert_fusion.5), channel_id=1, replica_groups=mesh['dp'=4,'row'=4,'col'=2] {'row'}, dimensions={0}, use_global_device_ids=true | all-gather | bytes 1105920 | tf_op jit(solution)/shard_map/all_gather | solution.py:447
  185.6 2.8 slice.161.up_ref
  188.4 4.4 fusion.14.grad_ref
  192.8 9.3 %mlp.1 = (bf16[768,538]{1,0:T(8,128)(2,1)}, bf16[768,538]{1,0:T(8,128)(2,1)}, bf16[768,1152]{1,0:T(8,128)(2,1)}, f32[1,538]{1,0:T(1,128)}) custom-call(s32[1]{0:T(128)} %bitcast.11.core_ref, bf16[768,1152]{1,0:T(8,128)(2,1)} %bitcast.166, bf16[1152,538]{1,0:T(8,128)(2,1)} %slice.161.up_ref, f32[1,538]{1,0:T(1,128)} %broadcast_in_dim.12.bias_ref, ...), custom_call_target="tpu_custom_call" | custom-call | tf_op jit(solution)/shard_map/mlp/pallas_call | solution.py:185
  210.3 5.2 %copy.169 = bf16[1152,1076]{1,0:T(8,128)(2,1)} copy(bf16[1152,1076]{0,1:T(8,128)(2,1)} %pad_maximum_fusion) | data formatting | bytes 4958208 | tf_op jit(solution)/shard_map/concatenate | solution.py:460
  215.5 2.9 dynamic-slice_bitcast_fusion.3
  221.8 4.1 fusion.90.w_ref
  228.3 8.1 %collective-permute-done.10 = bf16[288,1076]{1,0:T(8,128)(2,1)} collective-permute-done((bf16[288,1076]{1,0:T(8,128)(2,1)}, bf16[288,1076]{1,0:T(8,128)(2,1)}, u32[]{:S(2)}, u32[]{:S(2)}) %collective-permute-start.10) | collective-permute-done | bytes 619808 | tf_op jit(solution)/shard_map/ppermute | solution.py:67
  236.4 15.1 %collective-permute-done.11 = bf16[288,1076]{1,0:T(8,128)(2,1)} collective-permute-done((bf16[288,1076]{1,0:T(8,128)(2,1)}, bf16[288,1076]{1,0:T(8,128)(2,1)}, u32[]{:S(2)}, u32[]{:S(2)}) %collective-permute-start.11) | collective-permute-done | bytes 619808 | tf_op jit(solution)/shard_map/ppermute | solution.py:67
  251.5 2.9 fusion.13
  254.4 4.6 %all-to-all-start.5 = ((bf16[4,72,1076]{2,1,0:T(8,128)(2,1)}), bf16[4,72,1076]{2,1,0:T(8,128)(2,1)}, u32[]{:S(2)}, u32[]{:S(2)}) async-start(bf16[4,72,1076]{2,1,0:T(8,128)(2,1)} %bitcast.177), calls=%async_computation.8 | async-start | bytes 1327104 | tf_op jit(solution)/shard_map/all_to_all | solution.py:58
  259.0 7.4 %fusion.24 = f32[1152,768]{1,0:T(8,128)} fusion(bf16[768,538]{1,0:T(8,128)(2,1)} %get-tuple-element.37, bf16[1152,1152]{1,0:T(8,128)(2,1)S(1)} %fusion, bf16[1152,1076]{1,0:T(8,128)(2,1)} %bitcast.10), kind=kOutput, calls=%fused_computation.39 | convolution fusion | flops 2379939840 | bytes 8650752 | tf_op jit(solution)/shard_map/dot_general | solution.py:22
  266.4 4.8 %fusion.3 = bf16[1152,768]{1,0:T(8,128)(2,1)} fusion(f32[1152,768]{1,0:T(8,128)} %fusion.24, bf16[1152,1152]{1,0:T(8,128)(2,1)S(1)} %fusion, f32[96,1152]{1,0:T(8,128)S(1)} %get-tuple-element.183, s32[96]{0:T(128)S(1)} %copy-done.48), kind=kOutput, calls=%fused_computation.8 | convolution fusion | flops 426627072 | bytes 8405376 | tf_op jit(solution)/shard_map/dot_general | solution.py:22
  273.4 3.0 all-to-all-done.5
  281.9 18.9 %all_gather.59 = bf16[384,1152]{1,0:T(8,128)(2,1)S(1)} all-gather(bf16[96,1152]{1,0:T(8,128)(2,1)S(1)} %get-tuple-element.169), channel_id=1, replica_groups=mesh['dp'=4,'row'=4,'col'=2] {'row'}, dimensions={0}, use_global_device_ids=true | all-gather | bytes 1105920 | tf_op jit(solution)/shard_map/all_gather | solution.py:470
  307.3 10.5 %attend_back.1 = (bf16[432,768]{1,0:T(8,128)(2,1)}, f32[432,1]{1,0:T(8,128)}, bf16[1152,432]{1,0:T(8,128)(2,1)}, bf16[1152,144]{1,0:T(8,128)(2,1)}) custom-call(bf16[768,1152]{1,0:T(8,128)(2,1)} %bitcast.154, bf16[1152,144]{1,0:T(8,128)(2,1)} %slice.160.out_ref, bf16[2,3,72,768]{3,2,1,0:T(8,128)(2,1)} %get-tuple-element.39.qkv_ref, ...), custom_call_target="tpu_custom_call" | custom-call | tf_op jit(solution)/shard_map/attend_back/pallas_call | solution.py:238
  319.0 5.7 %first_back.1 = (bf16[4,160,768]{2,1,0:T(8,128)(2,1)}, bf16[4,160,768]{2,1,0:T(8,128)(2,1)}, f32[1152,2]{1,0:T(8,128)}) custom-call(s32[1]{0:T(128)} %bitcast.11.core_ref, bf16[1152,432]{1,0:T(8,128)(2,1)} %fusion.90.w_ref, bf16[432,768]{1,0:T(8,128)(2,1)} %get-tuple-element.41.grad_ref, bf16[1152,768]{1,0:T(8,128)(2,1)} %bitcast.152, ...), custom_call_target="tpu_custom_call" | custom-call | tf_op jit(solution)/shard_map/first_back/pallas_call | solution.py:283
  368.6 10.4 %collective-permute-done.15 = f32[13520]{0:T(1024)S(1)} collective-permute-done((f32[13520]{0:T(1024)S(1)}, f32[13520]{0:T(1024)S(1)}, u32[]{:S(2)}, u32[]{:S(2)}) %collective-permute-start.15) | collective-permute-done | bytes 54112 | tf_op jit(solution)/shard_map/ppermute | solution.py:93
  380.5 2.8 collective-permute-done.16
  404.1 3.5 all-to-all-start.4
  411.8 5.2 %all-to-all-done.4 = bf16[4,72,576]{2,1,0:T(8,128)(2,1)S(1)} async-done(((bf16[4,72,576]{2,1,0:T(8,128)(2,1)}), bf16[4,72,576]{2,1,0:T(8,128)(2,1)S(1)}, u32[]{:S(2)}, u32[]{:S(2)}) %all-to-all-start.4) | async-done | bytes 331808 | tf_op jit(solution)/shard_map/all_to_all | solution.py:58
  426.9 10.2 %reduce-scatter.8.cloned.1.call-done = bf16[160,768]{1,0:T(8,128)(2,1)} async-done(((bf16[640,768]{1,0:T(8,128)(2,1)}), bf16[160,768]{1,0:T(8,128)(2,1)}) %reduce-scatter.8.cloned.1.call-update) | async-done | bytes 245776 | tf_op jit(solution)/shard_map/reduce_scatter | solution.py:81
  (324 shorter events, 190.5 us)
Async XLA Ops:
  12.1 34.4 %copy-start.29 = (bf16[729,144]{0,1:T(8,128)(2,1)S(1)}, bf16[729,144]{0,1:T(8,128)(2,1)}, u32[]{:S(2)}) copy-start(bf16[729,144]{0,1:T(8,128)(2,1)} %param.21) | copy-start | bytes 629860
  13.1 53.1 %all-to-all-start = ((bf16[4,72,576]{2,1,0:T(8,128)(2,1)}), bf16[4,72,576]{2,1,0:T(8,128)(2,1)}, u32[]{:S(2)}, u32[]{:S(2)}) async-start(bf16[4,72,576]{2,1,0:T(8,128)(2,1)} %copy.146), calls=%async_computation | async-start | bytes 737280 | tf_op jit(solution)/shard_map/all_to_all | solution.py:58
  19.5 133.3 %all-gather.8.cloned.1.call-start = ((), (), s32[]{:S(2)}) async-start(), calls=%async_computation.10 | async-start | bytes 1990656 | tf_op jit(solution)/shard_map/all_gather | solution.py:406
  19.5 28.6 %copy-start.32 = (f32[11216]{0:T(1024)S(1)}, f32[11216]{0:T(1024)}, u32[]{:S(2)}) copy-start(f32[11216]{0:T(1024)} %param.37) | copy-start | bytes 134596
  68.5 23.3 %all-to-all-start.1 = ((bf16[4,288,576]{2,1,0:T(8,128)(2,1)}), bf16[4,288,576]{2,1,0:T(8,128)(2,1)}, u32[]{:S(2)}, u32[]{:S(2)}) async-start(bf16[4,288,576]{2,1,0:T(8,128)(2,1)} %broadcast_in_dim.10), calls=%async_computation.1 | async-start | bytes 2949120 | tf_op jit(solution)/shard_map/all_to_all | solution.py:49
  72.8 85.4 %reduce-scatter.4.cloned.1.call-start = ((), (), s32[]{:S(2)}) async-start(), calls=%async_computation.9 | async-start | bytes 1105920 | tf_op jit(solution)/shard_map/reduce_scatter | solution.py:81
  104.7 2.6 collective-permute-start
  118.7 21.1 %copy-start.21 = (bf16[729,144]{0,1:T(8,128)(2,1)S(1)}, bf16[729,144]{0,1:T(8,128)(2,1)}, u32[]{:S(2)}) copy-start(bf16[729,144]{0,1:T(8,128)(2,1)} %param.20) | copy-start | bytes 629860
  118.7 27.6 %all-to-all-start.2 = ((bf16[4,72,1076]{2,1,0:T(8,128)(2,1)}), bf16[4,72,1076]{2,1,0:T(8,128)(2,1)S(1)}, u32[]{:S(2)}, u32[]{:S(2)}) async-start(bf16[4,72,1076]{2,1,0:T(8,128)(2,1)} %copy.147), calls=%async_computation.2 | async-start | bytes 1327104 | tf_op jit(solution)/shard_map/all_to_all | solution.py:58
  148.1 37.6 %all-to-all-start.3 = ((bf16[4,288,1076]{2,1,0:T(8,128)(2,1)}), bf16[4,288,1076]{2,1,0:T(8,128)(2,1)}, u32[]{:S(2)}, u32[]{:S(2)}) async-start(bf16[4,288,1076]{2,1,0:T(8,128)(2,1)} %broadcast_in_dim.11), calls=%async_computation.3 | async-start | bytes 5308416 | tf_op jit(solution)/shard_map/all_to_all | solution.py:49
  152.7 126.0 %reduce-scatter.6.cloned.1.call-start = ((), (), s32[]{:S(2)}) async-start(), calls=%async_computation.11 | async-start | bytes 1105920 | tf_op jit(solution)/shard_map/reduce_scatter | solution.py:81
  204.4 21.6 %collective-permute-start.2 = (bf16[384,1152]{1,0:T(8,128)(2,1)}, bf16[384,1152]{1,0:T(8,128)(2,1)}, u32[]{:S(2)}, u32[]{:S(2)}) collective-permute-start(bf16[384,1152]{1,0:T(8,128)(2,1)} %slice.135), channel_id=1, source_target_pairs={{0,1},{1,0},{2,3},{3,2},{4,5},{5,4},{6,7},{7,6},{8,9},{9,8},{10,11... | collective-permute-start | bytes 2654216 | tf_op jit(solution)/shard_map/ppermute | solution.py:37
  218.3 18.1 %collective-permute-start.10 = (bf16[288,1076]{1,0:T(8,128)(2,1)}, bf16[288,1076]{1,0:T(8,128)(2,1)}, u32[]{:S(2)}, u32[]{:S(2)}) collective-permute-start(bf16[288,1076]{1,0:T(8,128)(2,1)} %get-tuple-element.184), channel_id=1, source_target_pairs={{0,8},{8,0},{16,24},{24,16},{1,9},{9,1},{17,25},{25,17},{2,10},{10... | collective-permute-start | bytes 1859336 | tf_op jit(solution)/shard_map/ppermute | solution.py:67
  220.1 31.4 %collective-permute-start.11 = (bf16[288,1076]{1,0:T(8,128)(2,1)}, bf16[288,1076]{1,0:T(8,128)(2,1)}, u32[]{:S(2)}, u32[]{:S(2)}) collective-permute-start(bf16[288,1076]{1,0:T(8,128)(2,1)} %get-tuple-element.186), channel_id=1, source_target_pairs={{0,16},{8,24},{16,0},{24,8},{1,17},{9,25},{17,1},{25,9},{2,18},{10... | collective-permute-start | bytes 1859336 | tf_op jit(solution)/shard_map/ppermute | solution.py:67
  221.6 30.0 %collective-permute-start.12 = (bf16[288,1076]{1,0:T(8,128)(2,1)}, bf16[288,1076]{1,0:T(8,128)(2,1)}, u32[]{:S(2)}, u32[]{:S(2)}) collective-permute-start(bf16[288,1076]{1,0:T(8,128)(2,1)} %get-tuple-element.185), channel_id=1, source_target_pairs={{0,24},{8,16},{16,8},{24,0},{1,25},{9,17},{17,9},{25,1},{2,26},{10... | collective-permute-start | bytes 1859336 | tf_op jit(solution)/shard_map/ppermute | solution.py:67
  254.4 22.0 %all-to-all-start.5 = ((bf16[4,72,1076]{2,1,0:T(8,128)(2,1)}), bf16[4,72,1076]{2,1,0:T(8,128)(2,1)}, u32[]{:S(2)}, u32[]{:S(2)}) async-start(bf16[4,72,1076]{2,1,0:T(8,128)(2,1)} %bitcast.177), calls=%async_computation.8 | async-start | bytes 1327104 | tf_op jit(solution)/shard_map/all_to_all | solution.py:58
  273.4 74.2 %collective-permute-start.1 = (bf16[576,768]{1,0:T(8,128)(2,1)}, bf16[576,768]{1,0:T(8,128)(2,1)}, u32[]{:S(2)}, u32[]{:S(2)}) collective-permute-start(bf16[576,768]{1,0:T(8,128)(2,1)} %dynamic-slice_bitcast_fusion), channel_id=1, source_target_pairs={{0,1},{1,0},{2,3},{3,2},{4,5},{5,4},{6,7},{7,6},{8,9},{9,8},{10,11... | collective-permute-start | bytes 2654216 | tf_op jit(solution)/shard_map/ppermute | solution.py:37
  343.2 17.4 %collective-permute-start.13 = (f32[13520]{0:T(1024)}, f32[13520]{0:T(1024)}, u32[]{:S(2)}, u32[]{:S(2)}) collective-permute-start(f32[13520]{0:T(1024)} %dynamic_update_slice.11), channel_id=1, source_target_pairs={{0,1},{1,0},{2,3},{3,2},{4,5},{5,4},{6,7},{7,6},{8,9},{9,8},{10,11... | collective-permute-start | bytes 162248 | tf_op jit(solution)/shard_map/ppermute | solution.py:93
  359.3 42.4 %collective-permute-start.7 = (bf16[288,576]{1,0:T(8,128)(2,1)}, bf16[288,576]{1,0:T(8,128)(2,1)}, u32[]{:S(2)}, u32[]{:S(2)}) collective-permute-start(bf16[288,576]{1,0:T(8,128)(2,1)} %get-tuple-element.188), channel_id=1, source_target_pairs={{0,8},{8,0},{16,24},{24,16},{1,9},{9,1},{17,25},{25,17},{2,10},{10... | collective-permute-start | bytes 995336 | tf_op jit(solution)/shard_map/ppermute | solution.py:67
  360.5 47.3 %collective-permute-start.6 = (bf16[4,160,768]{2,1,0:T(8,128)(2,1)}, bf16[4,160,768]{2,1,0:T(8,128)(2,1)}, u32[]{:S(2)}, u32[]{:S(2)}) collective-permute-start(bf16[4,160,768]{2,1,0:T(8,128)(2,1)} %get-tuple-element.43), channel_id=1, source_target_pairs={{0,1},{1,0},{2,3},{3,2},{4,5},{5,4},{6,7},{7,6},{8,9},{9,8},{10,11... | collective-permute-start | bytes 2949128 | tf_op jit(solution)/shard_map/ppermute | solution.py:37
  361.5 4.8 %collective-permute-start.14 = (f32[13520]{0:T(1024)S(1)}, f32[13520]{0:T(1024)S(1)}, u32[]{:S(2)}, u32[]{:S(2)}) collective-permute-start(f32[13520]{0:T(1024)S(1)} %add.516), channel_id=1, source_target_pairs={{0,2},{2,0},{4,6},{6,4},{1,3},{3,1},{5,7},{7,5},{8,10},{10,8},{12,... | collective-permute-start | bytes 162248 | tf_op jit(solution)/shard_map/ppermute | solution.py:93
  361.6 22.3 %collective-permute-start.3 = (bf16[144,768]{1,0:T(8,128)(2,1)S(1)}, bf16[144,768]{1,0:T(8,128)(2,1)S(1)}, u32[]{:S(2)}, u32[]{:S(2)}) collective-permute-start(bf16[144,768]{1,0:T(8,128)(2,1)S(1)} %get-tuple-element.193), channel_id=1, source_target_pairs={{0,2},{2,0},{4,6},{6,4},{1,3},{3,1},{5,7},{7,5},{8,10},{10,8},{12,... | collective-permute-start | bytes 663560 | tf_op jit(solution)/shard_map/ppermute | solution.py:67
  363.7 21.9 %collective-permute-start.4 = (bf16[144,768]{1,0:T(8,128)(2,1)S(1)}, bf16[144,768]{1,0:T(8,128)(2,1)S(1)}, u32[]{:S(2)}, u32[]{:S(2)}) collective-permute-start(bf16[144,768]{1,0:T(8,128)(2,1)S(1)} %get-tuple-element.195), channel_id=1, source_target_pairs={{0,4},{2,6},{4,0},{6,2},{1,5},{3,7},{5,1},{7,3},{8,12},{10,14},{12... | collective-permute-start | bytes 663560 | tf_op jit(solution)/shard_map/ppermute | solution.py:67
  366.3 12.7 %collective-permute-start.15 = (f32[13520]{0:T(1024)S(1)}, f32[13520]{0:T(1024)S(1)}, u32[]{:S(2)}, u32[]{:S(2)}) collective-permute-start(f32[13520]{0:T(1024)S(1)} %add.517), channel_id=1, source_target_pairs={{0,4},{2,6},{4,0},{6,2},{1,5},{3,7},{5,1},{7,3},{8,12},{10,14},{12... | collective-permute-start | bytes 162248 | tf_op jit(solution)/shard_map/ppermute | solution.py:93
  379.1 4.2 collective-permute-start.16
  383.3 18.5 %collective-permute-start.8 = (bf16[288,576]{1,0:T(8,128)(2,1)S(1)}, bf16[288,576]{1,0:T(8,128)(2,1)}, u32[]{:S(2)}, u32[]{:S(2)}) collective-permute-start(bf16[288,576]{1,0:T(8,128)(2,1)S(1)} %copy-done.28), channel_id=1, source_target_pairs={{0,16},{8,24},{16,0},{24,8},{1,17},{9,25},{17,1},{25,9},{2,18},{10... | collective-permute-start | bytes 995336 | tf_op jit(solution)/shard_map/ppermute | solution.py:67
  384.0 17.8 %collective-permute-start.9 = (bf16[288,576]{1,0:T(8,128)(2,1)S(1)}, bf16[288,576]{1,0:T(8,128)(2,1)}, u32[]{:S(2)}, u32[]{:S(2)}) collective-permute-start(bf16[288,576]{1,0:T(8,128)(2,1)S(1)} %copy-done.27), channel_id=1, source_target_pairs={{0,24},{8,16},{16,8},{24,0},{1,25},{9,17},{17,9},{25,1},{2,26},{10... | collective-permute-start | bytes 995336 | tf_op jit(solution)/shard_map/ppermute | solution.py:67
  385.6 11.9 %collective-permute-start.5 = (bf16[144,768]{1,0:T(8,128)(2,1)S(1)}, bf16[144,768]{1,0:T(8,128)(2,1)S(1)}, u32[]{:S(2)}, u32[]{:S(2)}) collective-permute-start(bf16[144,768]{1,0:T(8,128)(2,1)S(1)} %get-tuple-element.194), channel_id=1, source_target_pairs={{0,6},{2,4},{4,2},{6,0},{1,7},{3,5},{5,3},{7,1},{8,14},{10,12},{12... | collective-permute-start | bytes 663560 | tf_op jit(solution)/shard_map/ppermute | solution.py:67
  397.5 4.2 collective-permute-start.17
  404.1 12.9 %all-to-all-start.4 = ((bf16[4,72,576]{2,1,0:T(8,128)(2,1)}), bf16[4,72,576]{2,1,0:T(8,128)(2,1)S(1)}, u32[]{:S(2)}, u32[]{:S(2)}) async-start(bf16[4,72,576]{2,1,0:T(8,128)(2,1)} %bitcast.50), calls=%async_computation.7 | async-start | bytes 737280 | tf_op jit(solution)/shard_map/all_to_all | solution.py:58
  407.5 29.5 %reduce-scatter.8.cloned.1.call-start = ((), (), s32[]{:S(2)}) async-start(), calls=%async_computation.12 | async-start | bytes 1228800 | tf_op jit(solution)/shard_map/reduce_scatter | solution.py:81
  424.1 14.9 %copy-start.16 = (f32[144,768]{1,0:T(8,128)S(1)}, f32[144,768]{1,0:T(8,128)}, u32[]{:S(2)}) copy-start(f32[144,768]{1,0:T(8,128)} %convert_subtract_fusion.1) | copy-start | bytes 1327108
  (46 other events, 249.1 us)
Sparse Core Ops, SparseCore 0:
  47.4 26.6 all-gather.7
Sparse Core Ops, SparseCore 1:
  109.8 28.7 reduce-scatter.3
  228.4 24.4 reduce-scatter.5
  410.5 26.5 reduce-scatter.7
